TPU v7x, 32 devices: a whole 2x2x4 slice. The times are simulated.
32 devices in a mesh: replica: 8 (over y, x, core), shard: 4 (over z).
Axes of the slice: x: 2, y: 2, z: 4, core: 2. Of those that a mesh axis runs over, the one named last changes fastest.
Arguments:
- tokens: bfloat16 [32768, 768], P(('replica', 'shard')), may hold values from -6 to 6
- cotangent: bfloat16 [32768, 768], P(('replica', 'shard')), may hold values from -6 to 6
- segments: int32 [32, 1024], P(('replica', 'shard')), may hold values from 0 to 3, never falling along the last dimension, each value on 1 to 512 neighbouring positions
- routes: int32 [32768, 1], P(('replica', 'shard')), may hold values from 0 to 3; in each aligned block of 1024 rows (0 to 1023, 1024 to 2047, ...) at most 320 rows name the same one
- w_query: bfloat16 [768, 768], P('shard'), may hold values from -0.02734375 to 0.02734375
- w_key: bfloat16 [768, 768], P('shard'), may hold values from -0.21875 to 0.21875
- w_value: bfloat16 [768, 768], P('shard'), may hold values from -0.21875 to 0.21875
- w_output: bfloat16 [768, 768], P('shard'), may hold values from -1.75 to 1.75
- norm_attn: bfloat16 [768], P('shard'), may hold values from 0.5 to 1.5
- norm_ffn: bfloat16 [768], P('shard'), may hold values from 0.5 to 1.5
- w_router: bfloat16 [768, 4], P('shard'), may hold values from -0.15625 to 0.15625
- rel_bias: bfloat16 [32, 12], P('shard'), may hold values from -4 to 4
- expert_input_weight: bfloat16 [4, 768, 3072], P('shard'), may hold values from -0.21875 to 0.21875
- expert_output_weight: bfloat16 [4, 3072, 768], P('shard'), may hold values from -0.4375 to 0.4375
Outputs:
- mixed: bfloat16 [32768, 768], P(('replica', 'shard'))
- grad_tokens: float32 [32768, 768], P(('replica', 'shard'))
- grad_query: float32 [768, 768], P('shard')
- grad_key: float32 [768, 768], P('shard')
- grad_value: float32 [768, 768], P('shard')
- grad_output: float32 [768, 768], P('shard')
- grad_norm_attn: float32 [768], P('shard')
- grad_norm_ffn: float32 [768], P('shard')
- grad_router: float32 [768, 4], P('shard')
- grad_rel_bias: float32 [32, 12], P('shard')
- grad_expert_in: float32 [4, 768, 3072], P('shard')
- grad_expert_out: float32 [4, 3072, 768], P('shard')
Inputs may be any that keep to these rules, and one draw needn't show every extreme that they name: `segments`: within a sequence the segment numbers never fall; each of the 4 numbers covers 1 to 512 positions, and one covers exactly 512. `routes`: among the 1024 rows of one device no expert is named more than 320 times, and in some device's rows an expert is named exactly 320 times; every expert is named somewhere.
All inputs are finite; a program needn't handle non-finite values.
Results may differ from a plain program's by a relative error of at most 0.014.
Values may be sent and summed in bfloat16 or wider, within the bound.
No kernel may reach another device: no remote copies, remote signals or barrier semaphores. Data moves between devices by JAX's collectives and lax.ppermute only.
A program may use at most 320 MiB of HBM per device.

v0:
```python
from functools import partial
import jax
import jax.numpy as jnp
from jax import lax
from jax.sharding import PartitionSpec as P

highest = lax.Precision.HIGHEST
far_steps = (12, 16, 23, 32, 46, 64, 91)


def bucket_table(query_pos, key_pos):
    relative = key_pos[None, :] - query_pos[:, None]
    distance = jnp.abs(relative)
    beyond = jnp.zeros_like(distance)
    for threshold in far_steps:
        beyond = beyond + (distance >= threshold).astype(jnp.int32)
    inside = jnp.where(distance < 8, distance, 8 + beyond)
    return inside + 16 * (relative > 0).astype(jnp.int32)


def rms_norm(values_in, gain_vec):
    return (
        values_in
        * lax.rsqrt(jnp.mean(values_in * values_in, axis=-1, keepdims=True) + 1e-06)
        * gain_vec
    )


def block_scores(queries, key_rows, relative_bias_table, slot_indicators, allowed):
    raw_dot = jnp.einsum("qhe,khe->hqk", queries, key_rows, preferred_element_type=jnp.float32)
    relative_bias_term = jnp.einsum(
        "rni,rf->fni", slot_indicators, relative_bias_table, preferred_element_type=jnp.float32
    )
    scores = raw_dot + relative_bias_term
    return jnp.where(allowed[None], scores, -1e30)


def expert_forward(rows_in, first_all, second_all):
    before_activation = jnp.einsum(
        "ecd,edf->ecf", rows_in, first_all, preferred_element_type=jnp.float32
    )
    hidden = jax.nn.gelu(before_activation).astype(jnp.bfloat16)
    result = jnp.einsum(
        "ecf,efd->ecd", hidden, second_all, preferred_element_type=jnp.float32
    ).astype(jnp.bfloat16)
    return (before_activation, hidden, result)


def expert_backward(rows_in, before_activation, hidden, grad_result, first_all, second_all):
    grad_hidden = jnp.einsum(
        "ecd,efd->ecf", grad_result, second_all, preferred_element_type=jnp.float32
    )
    grad_second = jnp.einsum(
        "ecf,ecd->efd", hidden, grad_result, preferred_element_type=jnp.float32
    )
    grad_pre = jax.vjp(jax.nn.gelu, before_activation)[1](grad_hidden)[0].astype(jnp.bfloat16)
    grad_first = jnp.einsum("ecd,ecf->edf", rows_in, grad_pre, preferred_element_type=jnp.float32)
    grad_rows = jnp.einsum(
        "ecf,edf->ecd", grad_pre, first_all, preferred_element_type=jnp.float32
    ).astype(jnp.bfloat16)
    return (grad_first, grad_second, grad_rows)


def on_device(
    tokens,
    cotangent,
    segments,
    routes,
    w_query,
    w_key,
    w_value,
    w_output,
    norm_attn,
    norm_ffn,
    w_router,
    rel_bias,
    expert_input_weight,
    expert_output_weight,
):
    gathered = (
        lax.all_gather(w_query, "shard", axis=0, tiled=True),
        lax.all_gather(w_key, "shard", axis=0, tiled=True),
        lax.all_gather(w_value, "shard", axis=0, tiled=True),
        lax.all_gather(w_output, "shard", axis=0, tiled=True),
        lax.all_gather(norm_attn, "shard", axis=0, tiled=True),
        lax.all_gather(norm_ffn, "shard", axis=0, tiled=True),
        lax.all_gather(w_router, "shard", axis=0, tiled=True),
        lax.all_gather(rel_bias, "shard", axis=0, tiled=True),
    )
    (
        full_query,
        full_key,
        full_value,
        full_output,
        gain_one,
        gain_two,
        router,
        relative_bias_table,
    ) = gathered
    seq_count, length = segments.shape
    row_count, model_width = tokens.shape
    bucket_count, head_count = relative_bias_table.shape
    head_width = model_width // head_count
    experts = router.shape[1]
    qblock = min(512, length)
    positions = jnp.arange(length, dtype=jnp.int32)
    labels = jnp.arange(bucket_count, dtype=jnp.int32)

    def block_frame(which, offset):
        query_pos = positions[offset : offset + qblock]
        matches = bucket_table(query_pos, positions)[None] == labels[:, None, None]
        segment_row = segments[which]
        allowed = segment_row[offset : offset + qblock][:, None] == segment_row[None, :]
        return (matches, allowed)

    inputs = tokens.astype(jnp.float32)
    gain_one_f = gain_one.astype(jnp.float32)
    normed_one = rms_norm(inputs, gain_one_f).astype(jnp.bfloat16)

    def project(weight_mat):
        product = jnp.dot(normed_one, weight_mat, preferred_element_type=jnp.float32)
        return product.astype(jnp.bfloat16).reshape(seq_count, length, head_count, head_width)

    queries = project(full_query)
    key_rows = project(full_key)
    value_rows = project(full_value)
    pieces = []
    log_sums = []
    which = 0
    for offset in range(0, length, qblock):
        matches, allowed = block_frame(which, offset)
        scores = block_scores(
            queries[which, offset : offset + qblock],
            key_rows[which],
            relative_bias_table,
            matches.astype(jnp.bfloat16),
            allowed,
        )
        highest_score = jnp.max(scores, axis=-1, keepdims=True)
        shifted = jnp.exp(scores - highest_score)
        denominator = jnp.sum(shifted, axis=-1, keepdims=True)
        chances = (shifted / denominator).astype(jnp.bfloat16)
        log_sums.append(highest_score + jnp.log(denominator))
        pieces.append(
            jnp.einsum(
                "hqk,khe->qhe", chances, value_rows[which], preferred_element_type=jnp.float32
            )
        )
    attended = jnp.concatenate(pieces, 0).reshape(row_count, model_width).astype(jnp.bfloat16)
    branch = jnp.dot(attended, full_output, preferred_element_type=jnp.float32)
    middle = inputs + branch
    gain_two_f = gain_two.astype(jnp.float32)
    normed_two = rms_norm(middle, gain_two_f).astype(jnp.bfloat16)
    normed_two_f = normed_two.astype(jnp.float32)
    router_f = router.astype(jnp.float32)
    logits = jnp.dot(normed_two_f, router_f, precision=highest)
    gate_probs = jax.nn.softmax(logits, axis=-1)
    chosen = (routes == jnp.arange(experts, dtype=jnp.int32)[None, :]).astype(jnp.int32)
    chosen_f = chosen.astype(jnp.float32)
    chosen_gate = jnp.sum(gate_probs * chosen_f, axis=-1)
    slot_index = jnp.cumsum(chosen, axis=0) - chosen
    capacity = 5 * row_count // (4 * experts)
    slot_range = jnp.arange(capacity, dtype=jnp.int32)
    places = (
        (chosen.T[:, None, :] == 1) & (slot_index.T[:, None, :] == slot_range[None, :, None])
    ).astype(jnp.bfloat16)
    outgoing = jnp.einsum(
        "ect,td->ecd", places, normed_two, preferred_element_type=jnp.float32
    ).astype(jnp.bfloat16)
    arrived = lax.all_to_all(outgoing, "shard", split_axis=0, concat_axis=1, tiled=True)
    before_activation, hidden, result = expert_forward(
        arrived, expert_input_weight, expert_output_weight
    )
    returned = lax.all_to_all(result, "shard", split_axis=1, concat_axis=0, tiled=True)
    combined = jnp.einsum("ect,ecd->td", places, returned, preferred_element_type=jnp.float32)
    mixed_out = (middle + chosen_gate[:, None] * combined).astype(jnp.bfloat16)
    again = (
        lax.all_gather(w_query, "shard", axis=0, tiled=True),
        lax.all_gather(w_key, "shard", axis=0, tiled=True),
        lax.all_gather(w_value, "shard", axis=0, tiled=True),
        lax.all_gather(w_output, "shard", axis=0, tiled=True),
        lax.all_gather(norm_attn, "shard", axis=0, tiled=True),
        lax.all_gather(norm_ffn, "shard", axis=0, tiled=True),
        lax.all_gather(w_router, "shard", axis=0, tiled=True),
        lax.all_gather(rel_bias, "shard", axis=0, tiled=True),
    )
    (
        full_query,
        full_key,
        full_value,
        full_output,
        gain_one,
        gain_two,
        router,
        relative_bias_table,
    ) = again
    gain_one_f = gain_one.astype(jnp.float32)
    gain_two_f = gain_two.astype(jnp.float32)
    router_f = router.astype(jnp.float32)
    grad_final = cotangent.astype(jnp.float32)
    grad_gate = jnp.sum(grad_final * combined, axis=-1)
    scaled = (chosen_gate[:, None] * grad_final).astype(jnp.bfloat16)
    grad_slots = jnp.einsum(
        "ect,td->ecd", places, scaled, preferred_element_type=jnp.float32
    ).astype(jnp.bfloat16)
    grad_arrived = lax.all_to_all(grad_slots, "shard", split_axis=0, concat_axis=1, tiled=True)
    grad_first, grad_second, grad_rows = expert_backward(
        arrived, before_activation, hidden, grad_arrived, expert_input_weight, expert_output_weight
    )
    grad_back = lax.all_to_all(grad_rows, "shard", split_axis=1, concat_axis=0, tiled=True)
    grad_normed_two = jnp.einsum(
        "ect,ecd->td", places, grad_back, preferred_element_type=jnp.float32
    )
    grad_probs_gate = chosen_f * grad_gate[:, None]
    grad_logits = jax.vjp(partial(jax.nn.softmax, axis=-1), logits)[1](grad_probs_gate)[0]
    grad_router = jnp.dot(normed_two_f.T, grad_logits, precision=highest)
    grad_normed_two = grad_normed_two + jnp.dot(grad_logits, router_f.T, precision=highest)
    pull_two = jax.vjp(rms_norm, middle, gain_two_f)[1]
    grad_mid_norm, grad_gain_two = pull_two(grad_normed_two)
    grad_middle = grad_final + grad_mid_norm
    gradient_residual_branch = grad_middle.astype(jnp.bfloat16)
    grad_wout = jnp.einsum(
        "td,te->de", attended, gradient_residual_branch, preferred_element_type=jnp.float32
    )
    grad_attended = jnp.einsum(
        "te,de->td", gradient_residual_branch, full_output, preferred_element_type=jnp.float32
    )
    grad_attended = grad_attended.astype(jnp.bfloat16).reshape(
        seq_count, length, head_count, head_width
    )
    query_grads = []
    grad_table = jnp.zeros((bucket_count, head_count), jnp.float32)
    block_index = 0
    which = 0
    key_acc = jnp.zeros((length, head_count, head_width), jnp.float32)
    value_acc = jnp.zeros((length, head_count, head_width), jnp.float32)
    for offset in range(0, length, qblock):
        matches, allowed = block_frame(which, offset)
        query_part = queries[which, offset : offset + qblock]
        scores = block_scores(
            query_part, key_rows[which], relative_bias_table, matches.astype(jnp.bfloat16), allowed
        )
        chances = jnp.exp(scores - log_sums[block_index])
        grad_part = grad_attended[which, offset : offset + qblock]
        value_acc = value_acc + jnp.einsum(
            "hqk,qhe->khe",
            chances.astype(jnp.bfloat16),
            grad_part,
            preferred_element_type=jnp.float32,
        )
        grad_chances = jnp.einsum(
            "qhe,khe->hqk", grad_part, value_rows[which], preferred_element_type=jnp.float32
        )
        inner_sum = jnp.sum(chances * grad_chances, axis=-1, keepdims=True)
        grad_scores = chances * (grad_chances - inner_sum)
        grad_table = grad_table + jnp.einsum(
            "vsi,dsi->dv",
            grad_scores,
            matches.astype(jnp.float32),
            precision=highest,
            preferred_element_type=jnp.float32,
        )
        grad_raw = grad_scores.astype(jnp.bfloat16)
        query_grads.append(
            jnp.einsum(
                "hqk,khe->qhe", grad_raw, key_rows[which], preferred_element_type=jnp.float32
            )
        )
        key_acc = key_acc + jnp.einsum(
            "hqk,qhe->khe", grad_raw, query_part, preferred_element_type=jnp.float32
        )
        block_index = block_index + 1
    key_grads = [key_acc]
    value_grads = [value_acc]
    grad_q = jnp.concatenate(query_grads, 0).reshape(row_count, model_width).astype(jnp.bfloat16)
    grad_k = jnp.stack(key_grads).reshape(row_count, model_width).astype(jnp.bfloat16)
    grad_v = jnp.stack(value_grads).reshape(row_count, model_width).astype(jnp.bfloat16)
    grad_wq = jnp.einsum("td,te->de", normed_one, grad_q, preferred_element_type=jnp.float32)
    grad_wk = jnp.einsum("td,te->de", normed_one, grad_k, preferred_element_type=jnp.float32)
    grad_wv = jnp.einsum("td,te->de", normed_one, grad_v, preferred_element_type=jnp.float32)
    grad_normed_one = jnp.einsum(
        "te,de->td", grad_q, full_query, preferred_element_type=jnp.float32
    )
    grad_normed_one = grad_normed_one + jnp.einsum(
        "te,de->td", grad_k, full_key, preferred_element_type=jnp.float32
    )
    grad_normed_one = grad_normed_one + jnp.einsum(
        "te,de->td", grad_v, full_value, preferred_element_type=jnp.float32
    )
    pull_one = jax.vjp(rms_norm, inputs, gain_one_f)[1]
    grad_in_norm, grad_gain_one = pull_one(grad_normed_one)
    grad_inputs = grad_middle + grad_in_norm
    owned_grads = (
        lax.psum_scatter(grad_wq, "shard", scatter_dimension=0, tiled=True),
        lax.psum_scatter(grad_wk, "shard", scatter_dimension=0, tiled=True),
        lax.psum_scatter(grad_wv, "shard", scatter_dimension=0, tiled=True),
        lax.psum_scatter(grad_wout, "shard", scatter_dimension=0, tiled=True),
        lax.psum_scatter(grad_gain_one, "shard", scatter_dimension=0, tiled=True),
        lax.psum_scatter(grad_gain_two, "shard", scatter_dimension=0, tiled=True),
        lax.psum_scatter(grad_router, "shard", scatter_dimension=0, tiled=True),
        lax.psum_scatter(grad_table, "shard", scatter_dimension=0, tiled=True),
    )
    summed_grads = lax.psum(
        (
            owned_grads[0],
            owned_grads[1],
            owned_grads[2],
            owned_grads[3],
            owned_grads[4],
            owned_grads[5],
            owned_grads[6],
            owned_grads[7],
        ),
        "replica",
    )
    replica_parts = (
        lax.psum_scatter(grad_first, "replica", scatter_dimension=2, tiled=True),
        lax.psum_scatter(grad_second, "replica", scatter_dimension=1, tiled=True),
    )
    total_first, total_second = (
        lax.all_gather(replica_parts[0], "replica", axis=2, tiled=True),
        lax.all_gather(replica_parts[1], "replica", axis=1, tiled=True),
    )
    return (
        mixed_out,
        grad_inputs,
        summed_grads[0],
        summed_grads[1],
        summed_grads[2],
        summed_grads[3],
        summed_grads[4],
        summed_grads[5],
        summed_grads[6],
        summed_grads[7],
        total_first,
        total_second,
    )


def solution(mesh):
    placed = (
        P(("replica", "shard"), None),
        P(("replica", "shard"), None),
        P(("replica", "shard"), None),
        P(("replica", "shard"), None),
        P("shard", None),
        P("shard", None),
        P("shard", None),
        P("shard", None),
        P("shard"),
        P("shard"),
        P("shard", None),
        P("shard", None),
        P("shard", None, None),
        P("shard", None, None),
    )
    return jax.shard_map(
        on_device,
        mesh=mesh,
        in_specs=placed,
        out_specs=(
            P(("replica", "shard"), None),
            P(("replica", "shard"), None),
            P("shard", None),
            P("shard", None),
            P("shard", None),
            P("shard", None),
            P("shard"),
            P("shard"),
            P("shard", None),
            P("shard", None),
            P("shard", None, None),
            P("shard", None, None),
        ),
        check_vma=False,
    )
```

profile of v0, /device:TPU:0, one launch (start us, length us, event | category | flops | bytes accessed | tf_op | source)
XLA Modules:
  0.0 1068.2 jit_solution(8149581946401056184)
XLA Ops:
  13.6 13.6 %all-reduce.8 = (bf16[768]{0:T(1024)(128)(2,1)S(1)}, bf16[768]{0:T(1024)(128)(2,1)S(1)}) all-reduce(bf16[768]{0:T(1024)(128)(2,1)S(1)} %dynamic-update-slice, bf16[768]{0:T(1024)(128)(2,1)S(1)} %dynamic-update-slice.1), channel_id=1, replica_groups=mesh['replica'=8,'shard'=4] {'shard'}, use_global_device_ids=true, to_apply=%add | all-reduce | flops 1536 | bytes 6144
  29.9 12.1 %all_gather.42 = bf16[32,12]{1,0:T(8,128)(2,1)S(1)} all-gather(bf16[8,12]{1,0:T(8,128)(2,1)} %param.25), channel_id=1, replica_groups=mesh['replica'=8,'shard'=4] {'shard'}, dimensions={0}, use_global_device_ids=true | all-gather | bytes 960 | tf_op jit(solution)/shard_map/all_gather | solution.py:88
  54.6 16.3 %fusion.1 = f32[512,1024,12]{0,2,1:T(8,128)} fusion(s32[512,1024]{0,1:T(8,128)S(1)} %fusion.85, bf16[32,12]{1,0:T(8,128)(2,1)S(1)} %all_gather.42), kind=kOutput, calls=%fused_computation.2 | convolution fusion | flops 419430400 | bytes 27263744 | tf_op jit(solution)/shard_map/rni,rf->fni/dot_general | solution.py:31
  70.9 29.9 %copy.81 = f32[512,1024,12]{1,0,2:T(8,128)} copy(f32[512,1024,12]{0,2,1:T(8,128)} %fusion.1) | data formatting | bytes 50331648 | tf_op jit(solution)/shard_map/rni,rf->fni/dot_general | solution.py:31
  100.9 16.5 %fusion.3 = f32[512,1024,12]{0,2,1:T(8,128)} fusion(s32[512,1024]{0,1:T(8,128)S(1)} %fusion.84, bf16[32,12]{1,0:T(8,128)(2,1)S(1)} %all_gather.42), kind=kOutput, calls=%fused_computation.5 | convolution fusion | flops 419430400 | bytes 27263744 | tf_op jit(solution)/shard_map/rni,rf->fni/dot_general | solution.py:31
  117.4 30.6 %copy.80 = f32[512,1024,12]{1,0,2:T(8,128)} copy(f32[512,1024,12]{0,2,1:T(8,128)} %fusion.3) | data formatting | bytes 50331648 | tf_op jit(solution)/shard_map/rni,rf->fni/dot_general | solution.py:31
  156.3 16.6 %fusion.161 = (f32[12,512]{1,0:T(8,128)S(1)}, f32[12,512,1024]{2,1,0:T(8,128)}) fusion(f32[512,1024,12]{1,0,2:T(8,128)} %copy.81, bf16[1024,12,64]{0,2,1:T(8,128)(2,1)S(1)} %bitcast.170, bf16[1,1024,12,64]{1,3,2,0:T(8,128)(2,1)} %bitcast.190, pred[512,1024]{1,0:T(8,128)(4,1)} %get-tuple-element.82), kind=kOutput, calls=%fused_computation.199 | convolution fusion | flops 824174592 | bytes 53239808 | tf_op jit(solution)/shard_map/qhe,khe->hqk/dot_general | solution.py:30
  172.9 11.4 %fusion.11 = f32[12,512]{1,0:T(8,128)S(1)} fusion(f32[12,512,1024]{2,1,0:T(8,128)} %get-tuple-element.88, f32[12,512]{1,0:T(8,128)S(1)} %get-tuple-element.87), kind=kLoop, calls=%fused_computation.27 | loop fusion | flops 12576768 | bytes 25214976 | tf_op jit(solution)/shard_map/reduce_sum | solution.py:141
  187.2 12.0 %fusion.133 = bf16[512,12,64]{0,2,1:T(8,128)(2,1)} fusion(bf16[1024,12,64]{0,2,1:T(8,128)(2,1)S(1)} %bitcast.180, f32[12,512,1024]{2,1,0:T(8,128)} %get-tuple-element.88, f32[12,512]{1,0:T(8,128)S(1)} %fusion.11, f32[12,512]{1,0:T(8,128)S(1)} %get-tuple-element.87), kind=kOutput, calls=%fused_computation.151 | convolution fusion | flops 824573952 | bytes 27574272 | tf_op jit(solution)/shard_map/hqk,khe->qhe/dot_general | solution.py:145
  199.1 15.7 %fusion.162 = (f32[12,512]{1,0:T(8,128)S(1)}, f32[12,512,1024]{2,1,0:T(8,128)}) fusion(f32[512,1024,12]{1,0,2:T(8,128)} %copy.80, bf16[1024,12,64]{0,2,1:T(8,128)(2,1)S(1)} %bitcast.171, bf16[1,1024,12,64]{1,3,2,0:T(8,128)(2,1)S(1)} %bitcast.191, pred[512,1024]{1,0:T(8,128)(4,1)} %get-tuple-element.81), kind=kOutput, calls=%fused_computation.200 | convolution fusion | flops 824174592 | bytes 53239808 | tf_op jit(solution)/shard_map/qhe,khe->hqk/dot_general | solution.py:30
  214.8 11.0 %fusion.10 = f32[12,512]{1,0:T(8,128)S(1)} fusion(f32[12,512,1024]{2,1,0:T(8,128)} %get-tuple-element.90, f32[12,512]{1,0:T(8,128)S(1)} %get-tuple-element.89), kind=kLoop, calls=%fused_computation.26 | loop fusion | flops 12576768 | bytes 25214976 | tf_op jit(solution)/shard_map/reduce_sum | solution.py:141
  225.9 10.5 fusion.132
  245.1 44.4 %all_to_all.42 = bf16[4,320,768]{2,1,0:T(8,128)(2,1)S(1)} all-to-all(bf16[4,320,768]{2,1,0:T(8,128)(2,1)S(1)} %fusion.104), channel_id=1, replica_groups=mesh['replica'=8,'shard'=4] {'shard'}, dimensions={0} | all-to-all | bytes 3932160 | tf_op jit(solution)/shard_map/all_to_all | solution.py:170
  290.8 6.4 fusion.51
  297.3 9.6 fusion.70
  306.9 15.1 %copy.116 = bf16[1,1280,768]{2,0,1:T(2,128)(2,1)} copy(bf16[1,1280,768]{2,1,0:T(8,128)(2,1)S(1)} %fusion.70) | data formatting | bytes 3932160 | tf_op jit(solution)/shard_map/convert_element_type | solution.py:45
  322.5 13.7 %reduce.2 = bf16[1280,768]{1,0:T(8,128)(2,1)} reduce(bf16[1280,1,768]{2,1,0:T(2,128)(2,1)} %bitcast.174, bf16[]{:T(256)} %broadcast.378), dimensions={1}, to_apply=%bitcast.168.reduce_sub_computation | reduce | bytes 3932162
  340.2 4.5 all-to-all-start.1
  344.7 48.8 %all-gather = bf16[4,192,4]{1,2,0:T(4,128)(2,1)S(1)} all-gather(bf16[1,192,4]{1,2,0:T(4,128)(2,1)S(1)} %bitcast.216), channel_id=1, replica_groups=mesh['replica'=8,'shard'=4] {'shard'}, dimensions={0}, use_global_device_ids=true | all-gather | bytes 7680 | tf_op jit(solution)/shard_map/all_gather | solution.py:87
  398.1 4.8 reshape.409
  412.3 44.4 %all_to_all.43 = bf16[4,320,768]{2,1,0:T(8,128)(2,1)S(1)} all-to-all(bf16[4,320,768]{2,1,0:T(8,128)(2,1)S(1)} %fusion.107), channel_id=1, replica_groups=mesh['replica'=8,'shard'=4] {'shard'}, dimensions={0} | all-to-all | bytes 3932160 | tf_op jit(solution)/shard_map/all_to_all | solution.py:206
  458.0 10.0 convolution_bitcast_fusion
  468.1 19.0 %fusion.20 = bf16[1280,3072]{1,0:T(8,128)(2,1)S(1)} fusion(f32[1280,3072]{1,0:T(8,128)} %copy-done.54, bf16[1280,768]{1,0:T(8,128)(2,1)} %bitcast.197, bf16[1,3072,768]{2,1,0:T(8,128)(2,1)} %param.27), kind=kOutput, calls=%fused_computation.36 | convolution fusion | flops 6118440960 | bytes 30277632 | tf_op jit(solution)/shard_map/ecd,efd->ecf/dot_general | solution.py:50
  490.3 8.8 convolution_bitcast_fusion.1
  499.1 10.4 fusion.73
  509.5 15.3 %copy.115 = bf16[1,1280,768]{2,0,1:T(2,128)(2,1)} copy(bf16[1,1280,768]{2,1,0:T(8,128)(2,1)S(1)} %fusion.73) | data formatting | bytes 3932160 | tf_op jit(solution)/shard_map/convert_element_type | solution.py:60
  524.8 13.8 %reduce.3 = bf16[1280,768]{1,0:T(8,128)(2,1)} reduce(bf16[1280,1,768]{2,1,0:T(2,128)(2,1)} %bitcast.175, bf16[]{:T(256)} %broadcast.378), dimensions={1}, to_apply=%bitcast.167.reduce_sub_computation | reduce | bytes 3932162
  542.5 4.4 all-to-all-start.3
  550.7 39.7 %all-to-all-done.3 = bf16[4,2,122880]{2,1,0:T(2,128)(2,1)} async-done(((bf16[4,2,122880]{2,1,0:T(2,128)(2,1)}), bf16[4,2,122880]{2,1,0:T(2,128)(2,1)}, u32[]{:S(2)}, u32[]{:S(2)}) %all-to-all-start.3) | async-done | bytes 1966112 | tf_op jit(solution)/shard_map/all_to_all | solution.py:210
  590.4 5.1 reshape.411
  613.6 11.1 %fusion.21 = f32[12,64,1024]{2,1,0:T(8,128)S(1)} fusion(f32[12,512,1024]{2,1,0:T(8,128)} %get-tuple-element.88, f32[12,512]{1,0:T(8,128)S(1)} %log_add_fusion, bf16[1,1024,12,64]{1,3,2,0:T(8,128)(2,1)S(1)} %bitcast.186), kind=kOutput, calls=%fused_computation.38 | convolution fusion | flops 817889280 | bytes 29130752 | tf_op jit(solution)/shard_map/hqk,qhe->khe/dot_general | solution.py:245
  624.8 10.7 %add_convert_fusion = bf16[12,64,1024]{2,1,0:T(8,128)(2,1)S(1)} fusion(f32[12,64,1024]{2,1,0:T(8,128)S(1)} %fusion.21, f32[12,512,1024]{2,1,0:T(8,128)} %get-tuple-element.90, f32[12,512]{1,0:T(8,128)S(1)} %log_add_fusion.1, bf16[1,1024,12,64]{1,3,2,0:T(8,128)(2,1)S(1)} %bitcast.187), kind=kOutput, calls=%fused_computation.95 | convolution fusion | flops 819462144 | bytes 30703616 | tf_op jit(solution)/shard_map/hqk,qhe->khe/dot_general | solution.py:245
  639.5 16.2 %multiply_reduce_fusion = (f32[12,512]{1,0:T(8,128)S(1)}, f32[12,512,1024]{2,1,0:T(8,128)}) fusion(f32[12,512,1024]{2,1,0:T(8,128)} %get-tuple-element.88, f32[12,512]{1,0:T(8,128)S(1)} %log_add_fusion, bf16[1024,12,64]{0,2,1:T(8,128)(2,1)S(1)} %bitcast.182, bf16[1,1024,12,64]{1,3,2,0:T(8,128)(2,1)} %bitcast.188), kind=kOutput, calls=%fused_computation.15 | convolution fusion | flops 824174592 | bytes 52740096 | tf_op jit(solution)/shard_map/qhe,khe->hqk/dot_general | solution.py:251
  655.7 16.0 %multiply_reduce_fusion.1 = (f32[12,512]{1,0:T(8,128)S(1)}, f32[12,512,1024]{2,1,0:T(8,128)}) fusion(f32[12,512,1024]{2,1,0:T(8,128)} %get-tuple-element.90, f32[12,512]{1,0:T(8,128)S(1)} %log_add_fusion.1, bf16[1024,12,64]{0,2,1:T(8,128)(2,1)S(1)} %bitcast.183, bf16[1,1024,12,64]{1,3,2,0:T(8,128)(2,1)} %bitcast.189), kind=kOutput, calls=%fused_computation.18 | convolution fusion | flops 824174592 | bytes 52740096 | tf_op jit(solution)/shard_map/qhe,khe->hqk/dot_general | solution.py:251
  671.8 26.1 %subtract_multiply_fusion = f32[12,512,1024]{2,1,0:T(8,128)} fusion(f32[12,512,1024]{2,1,0:T(8,128)} %get-tuple-element.99, f32[12,512,1024]{2,1,0:T(8,128)} %get-tuple-element.88, f32[12,512]{1,0:T(8,128)S(1)} %get-tuple-element.98, f32[12,512]{1,0:T(8,128)S(1)} %log_add_fusion), kind=kLoop, calls=%fused_computation.14 | loop fusion | flops 18874368 | bytes 75546624 | tf_op jit(solution)/shard_map/mul | solution.py:255
  697.9 13.4 %fusion.126 = bf16[512,12,64]{0,2,1:T(8,128)(2,1)} fusion(bf16[1024,12,64]{0,2,1:T(8,128)(2,1)S(1)} %bitcast.172, f32[12,512,1024]{2,1,0:T(8,128)} %subtract_multiply_fusion), kind=kOutput, calls=%fused_computation.148 | convolution fusion | flops 811991040 | bytes 27525120 | tf_op jit(solution)/shard_map/hqk,khe->qhe/dot_general | solution.py:265
  711.3 26.0 %subtract_multiply_fusion.1 = f32[12,512,1024]{2,1,0:T(8,128)} fusion(f32[12,512,1024]{2,1,0:T(8,128)} %get-tuple-element.101, f32[12,512,1024]{2,1,0:T(8,128)} %get-tuple-element.90, f32[12,512]{1,0:T(8,128)S(1)} %get-tuple-element.100, f32[12,512]{1,0:T(8,128)S(1)} %log_add_fusion.1), kind=kLoop, calls=%fused_computation.17 | loop fusion | flops 18874368 | bytes 75546624 | tf_op jit(solution)/shard_map/mul | solution.py:255
  737.3 13.1 %fusion.129 = bf16[512,12,64]{0,2,1:T(8,128)(2,1)} fusion(bf16[1024,12,64]{0,2,1:T(8,128)(2,1)S(1)} %bitcast.173, f32[12,512,1024]{2,1,0:T(8,128)} %subtract_multiply_fusion.1), kind=kOutput, calls=%fused_computation.149 | convolution fusion | flops 811991040 | bytes 27525120 | tf_op jit(solution)/shard_map/hqk,khe->qhe/dot_general | solution.py:265
  756.0 10.9 %fusion.29 = f32[12,64,1024]{2,1,0:T(8,128)S(1)} fusion(f32[12,512,1024]{2,1,0:T(8,128)} %subtract_multiply_fusion, bf16[1,1024,12,64]{1,3,2,0:T(8,128)(2,1)S(1)} %bitcast.192), kind=kOutput, calls=%fused_computation.44 | convolution fusion | flops 811597824 | bytes 29097984 | tf_op jit(solution)/shard_map/hqk,qhe->khe/dot_general | solution.py:269
  766.9 10.7 %add_convert_fusion.1 = bf16[12,64,1024]{2,1,0:T(8,128)(2,1)S(1)} fusion(f32[12,64,1024]{2,1,0:T(8,128)S(1)} %fusion.29, f32[12,512,1024]{2,1,0:T(8,128)} %subtract_multiply_fusion.1, bf16[1,1024,12,64]{1,3,2,0:T(8,128)(2,1)S(1)} %bitcast.193), kind=kOutput, calls=%fused_computation.97 | convolution fusion | flops 813170688 | bytes 30670848 | tf_op jit(solution)/shard_map/hqk,qhe->khe/dot_general | solution.py:269
  785.4 31.0 %copy.94 = f32[12,512,1024]{1,0,2:T(8,128)} copy(f32[12,512,1024]{2,1,0:T(8,128)} %subtract_multiply_fusion) | data formatting | bytes 50331648 | tf_op jit(solution)/shard_map/mul | solution.py:255
  816.4 31.0 %copy.93 = f32[12,512,1024]{1,0,2:T(8,128)} copy(f32[12,512,1024]{2,1,0:T(8,128)} %subtract_multiply_fusion.1) | data formatting | bytes 50331648 | tf_op jit(solution)/shard_map/mul | solution.py:255
  862.5 38.0 %fusion.134 = f32[32,12]{1,0:T(8,128)S(1)} fusion(f32[12,512,1024]{1,0,2:T(8,128)} %copy.93, s32[512,1024]{0,1:T(8,128)S(1)} %copy-done.3), kind=kOutput, calls=%fused_computation.152 | convolution fusion | flops 2432696320 | bytes 27264512 | tf_op jit(solution)/shard_map/vsi,dsi->dv/dot_general | solution.py:256
  902.0 39.7 %fusion.136 = f32[32,12]{1,0:T(8,128)S(1)} fusion(f32[32,12]{1,0:T(8,128)S(1)} %fusion.134, f32[12,512,1024]{1,0,2:T(8,128)} %copy.94, s32[512,1024]{0,1:T(8,128)S(1)} %copy-done.1), kind=kOutput, calls=%fused_computation.154 | convolution fusion | flops 2432696832 | bytes 27266048 | tf_op jit(solution)/shard_map/vsi,dsi->dv/dot_general | solution.py:256
  941.8 17.0 %all-reduce.7 = (f32[768]{0:T(1024)S(1)}, f32[768]{0:T(1024)S(1)}, f32[32,12]{1,0:T(8,128)S(1)}) all-reduce(f32[768]{0:T(1024)S(1)} %get-tuple-element.62, f32[768]{0:T(1024)S(1)} %copy-done.47, f32[32,12]{1,0:T(8,128)S(1)} %fusion.136), channel_id=6, replica_groups=mesh['replica'=8,'shard'=4] {'shard'}, use_global_device_ids=true, to_apply=%region_26.27.clone | all-reduce | flops 1920 | bytes 15360
  958.9 22.7 %all-reduce.5 = (f32[192]{0:T(256)}, f32[192]{0:T(256)}, f32[192,4]{0,1:T(4,128)}, f32[8,12]{1,0:T(8,128)}) all-reduce(f32[192]{0:T(256)S(1)} %dynamic-slice.3, f32[192]{0:T(256)S(1)} %dynamic-slice.5, f32[192,4]{0,1:T(4,128)S(1)} %copy.108, ...), channel_id=1, replica_groups=mesh['replica'=8,'shard'=4] {'replica'}, use_global_device_ids=true, to_apply=%region_27.28 | all-reduce | flops 1248 | bytes 9984 | tf_op jit(solution)/shard_map/psum | solution.py:303
  981.6 60.0 %all-reduce.11.cloned.1.call-done = (f32[192,768]{1,0:T(8,128)}, f32[192,768]{1,0:T(8,128)}, f32[192,768]{1,0:T(8,128)}, f32[192,768]{1,0:T(8,128)}) async-done(((f32[192,768]{1,0:T(8,128)}, f32[192,768]{1,0:T(8,128)}, f32[192,768]{1,0:T(8,128)}, f32[192,768]{1,0:T(8,128)}), (f32[192,768]{1,0:T(8,128)}, f32[192,768]{1,0:T(8,128)}, f32[192,768]{1,0:T(8,128)}, ...) | async-done | bytes 2359312 | tf_op jit(solution)/shard_map/psum | solution.py:303
  1048.2 9.2 copy.129
  (255 shorter events, 133.8 us)
Async XLA Ops:
  7.2 142.4 %all-gather.10.cloned.1.call-start = ((), (), s32[]{:S(2)}) async-start(), calls=%async_computation.12 | async-start | bytes 1474560 | tf_op jit(solution)/shard_map/all_gather | solution.py:81
  7.9 145.6 %all-gather.12.cloned.1.call-start = ((), (), s32[]{:S(2)}) async-start(), calls=%async_computation.13 | async-start | bytes 1474560 | tf_op jit(solution)/shard_map/all_gather | solution.py:82
  8.7 175.6 %all-gather.8.cloned.1.call-start = ((), (), s32[]{:S(2)}) async-start(), calls=%async_computation.11 | async-start | bytes 1474560 | tf_op jit(solution)/shard_map/all_gather | solution.py:83
  9.4 228.3 %all-gather.14.cloned.1.call-start = ((), (), s32[]{:S(2)}) async-start(), calls=%async_computation.14 | async-start | bytes 1474560 | tf_op jit(solution)/shard_map/all_gather | solution.py:84
  27.3 157.0 %copy-start.40 = (f32[768]{0:T(1024)}, f32[768]{0:T(1024)S(1)}, u32[]{:S(2)}) copy-start(f32[768]{0:T(1024)S(1)} %convert_element_type.284) | copy-start | bytes 9220
  49.1 135.2 %copy-start.42 = (f32[1024]{0:T(1024)}, f32[1024]{0:T(1024)S(1)}, u32[]{:S(2)}) copy-start(f32[1024]{0:T(1024)S(1)} %fusion.146) | copy-start | bytes 12292
  51.2 49.7 %copy-start.2 = (s32[512,1024]{0,1:T(8,128)}, s32[512,1024]{0,1:T(8,128)S(1)}, u32[]{:S(2)}) copy-start(s32[512,1024]{0,1:T(8,128)S(1)} %fusion.84) | copy-start | bytes 6291460
  117.4 30.6 %copy-start.46 = (s32[1,1024]{1,0:T(1,128)S(1)}, s32[1,1024]{1,0:T(1,128)}, u32[]{:S(2)}) copy-start(s32[1,1024]{1,0:T(1,128)} %param.16) | copy-start | bytes 12292
  117.4 32.2 %copy-start.7 = (bf16[1024,768]{0,1:T(8,128)(2,1)S(1)}, bf16[1024,768]{0,1:T(8,128)(2,1)}, u32[]{:S(2)}) copy-start(bf16[1024,768]{0,1:T(8,128)(2,1)} %copy-done.6) | copy-start | bytes 4718596
  156.3 42.8 %copy-start.4 = (bf16[1024,768]{0,1:T(8,128)(2,1)}, bf16[1024,768]{0,1:T(8,128)(2,1)S(1)}, u32[]{:S(2)}) copy-start(bf16[1024,768]{0,1:T(8,128)(2,1)S(1)} %convolution_convert_fusion.1) | copy-start | bytes 4718596
  172.9 14.2 %copy-start.34 = (f32[12,512]{1,0:T(8,128)}, f32[12,512]{1,0:T(8,128)S(1)}, u32[]{:S(2)}) copy-start(f32[12,512]{1,0:T(8,128)S(1)} %get-tuple-element.87) | copy-start | bytes 73732
  187.1 12.0 %copy-start.12 = (bf16[1024,768]{0,1:T(8,128)(2,1)}, bf16[1024,768]{0,1:T(8,128)(2,1)S(1)}, u32[]{:S(2)}) copy-start(bf16[1024,768]{0,1:T(8,128)(2,1)S(1)} %convolution_convert_fusion.3) | copy-start | bytes 4718596
  187.1 12.0 %copy-start.21 = (bf16[1024,768]{0,1:T(8,128)(2,1)S(1)}, bf16[1024,768]{0,1:T(8,128)(2,1)}, u32[]{:S(2)}) copy-start(bf16[1024,768]{0,1:T(8,128)(2,1)} %convolution_convert_fusion.2) | copy-start | bytes 4718596
  214.8 11.0 %copy-start.13 = (bf16[1024,768]{0,1:T(8,128)(2,1)S(1)}, bf16[1024,768]{0,1:T(8,128)(2,1)}, u32[]{:S(2)}) copy-start(bf16[1024,768]{0,1:T(8,128)(2,1)} %copy-done.12) | copy-start | bytes 4718596
  225.9 10.5 copy-start.32
  237.7 53.1 %slice-start.5 = ((s8[4718592]{0:T(1024)(128)(4,1)}), s8[4194304]{0:T(1024)(128)(4,1)S(1)}, s32[]{:S(2)}) async-start(s8[4718592]{0:T(1024)(128)(4,1)} %bitcast.219), calls=%async_computation.30 | async-start | bytes 8388608
  242.4 48.4 %slice-start.6 = ((s8[4718592]{0:T(1024)(128)(4,1)}), s8[524288]{0:T(1024)(128)(4,1)S(1)}, s32[]{:S(2)}) async-start(s8[4718592]{0:T(1024)(128)(4,1)} %bitcast.219), calls=%async_computation.31 | async-start | bytes 1048576
  242.4 54.9 %slice-start.3 = ((s8[4718592]{0:T(1024)(128)(4,1)}), s8[4194304]{0:T(1024)(128)(4,1)S(1)}, s32[]{:S(2)}) async-start(s8[4718592]{0:T(1024)(128)(4,1)} %bitcast.217), calls=%async_computation.28 | async-start | bytes 8388608
  297.3 9.6 copy-start.54
  336.2 8.4 copy-start.50
  340.2 58.0 %all-to-all-start.1 = ((bf16[4,2,122880]{2,1,0:T(2,128)(2,1)}), bf16[4,2,122880]{2,1,0:T(2,128)(2,1)}, u32[]{:S(2)}, u32[]{:S(2)}) async-start(bf16[4,2,122880]{2,1,0:T(2,128)(2,1)} %reshape.408), calls=%async_computation.1 | async-start | bytes 3932160 | tf_op jit(solution)/shard_map/all_to_all | solution.py:174
  344.6 437.1 %reduce-scatter.20.cloned.1.call-start = ((), (), s32[]{:S(2)}) async-start(), calls=%async_computation.21 | async-start | bytes 10616832 | tf_op jit(solution)/shard_map/reduce_scatter | solution.py:318
  405.5 52.5 %slice-start.7 = ((s8[15728640]{0:T(1024)(128)(4,1)}), s8[4194304]{0:T(1024)(128)(4,1)S(1)}, s32[]{:S(2)}) async-start(s8[15728640]{0:T(1024)(128)(4,1)} %bitcast.221), calls=%async_computation.32 | async-start | bytes 8388608
  405.5 52.5 %slice-start.8 = ((s8[15728640]{0:T(1024)(128)(4,1)}), s8[4194304]{0:T(1024)(128)(4,1)S(1)}, s32[]{:S(2)}) async-start(s8[15728640]{0:T(1024)(128)(4,1)} %bitcast.221), calls=%async_computation.33 | async-start | bytes 8388608
  409.6 48.4 %slice-start.9 = ((s8[15728640]{0:T(1024)(128)(4,1)}), s8[4194304]{0:T(1024)(128)(4,1)S(1)}, s32[]{:S(2)}) async-start(s8[15728640]{0:T(1024)(128)(4,1)} %bitcast.221), calls=%async_computation.34 | async-start | bytes 8388608
  409.6 48.4 %slice-start.10 = ((s8[15728640]{0:T(1024)(128)(4,1)}), s8[3145728]{0:T(1024)(128)(4,1)S(1)}, s32[]{:S(2)}) async-start(s8[15728640]{0:T(1024)(128)(4,1)} %bitcast.221), calls=%async_computation.35 | async-start | bytes 6291456
  468.1 314.2 %reduce-scatter.18.cloned.1.call-start = ((), (), s32[]{:S(2)}) async-start(), calls=%async_computation.19 | async-start | bytes 10616832 | tf_op jit(solution)/shard_map/reduce_scatter | solution.py:317
  468.1 22.2 %copy-start.25 = (bf16[4,320,768]{2,1,0:T(8,128)(2,1)S(1)}, bf16[4,320,768]{2,1,0:T(8,128)(2,1)}, u32[]{:S(2)}) copy-start(bf16[4,320,768]{2,1,0:T(8,128)(2,1)} %copy-done.24) | copy-start | bytes 5898244
  538.6 8.4 copy-start.38
  542.5 47.9 %all-to-all-start.3 = ((bf16[4,2,122880]{2,1,0:T(2,128)(2,1)}), bf16[4,2,122880]{2,1,0:T(2,128)(2,1)}, u32[]{:S(2)}, u32[]{:S(2)}) async-start(bf16[4,2,122880]{2,1,0:T(2,128)(2,1)} %reshape.410), calls=%async_computation.3 | async-start | bytes 3932160 | tf_op jit(solution)/shard_map/all_to_all | solution.py:210
  546.9 237.4 %reduce-scatter.22.cloned.1.call-start = ((), (), s32[]{:S(2)}) async-start(), calls=%async_computation.23 | async-start | bytes 491520
  550.6 349.8 %reduce-scatter.16.cloned.1.call-start = ((), (), s32[]{:S(2)}) async-start(), calls=%async_computation.18 | async-start | bytes 2949120 | tf_op jit(solution)/shard_map/reduce_scatter | solution.py:297
  610.2 290.2 %reduce-scatter.14.cloned.1.call-start = ((), (), s32[]{:S(2)}) async-start(), calls=%async_computation.17 | async-start | bytes 2949120 | tf_op jit(solution)/shard_map/reduce_scatter | solution.py:296
  613.6 11.2 %copy-start.20 = (bf16[1024,768]{0,1:T(8,128)(2,1)}, bf16[1024,768]{0,1:T(8,128)(2,1)S(1)}, u32[]{:S(2)}) copy-start(bf16[1024,768]{0,1:T(8,128)(2,1)S(1)} %convolution_convert_fusion) | copy-start | bytes 4718596
  624.8 11.9 %copy-start.8 = (bf16[1024,768]{0,1:T(8,128)(2,1)S(1)}, bf16[1024,768]{0,1:T(8,128)(2,1)}, u32[]{:S(2)}) copy-start(bf16[1024,768]{0,1:T(8,128)(2,1)} %copy-done.6) | copy-start | bytes 4718596
  624.8 11.9 %copy-start.41 = (f32[768]{0:T(1024)S(1)}, f32[768]{0:T(1024)}, u32[]{:S(2)}) copy-start(f32[768]{0:T(1024)} %copy-done.40) | copy-start | bytes 9220
  624.8 11.9 %copy-start.43 = (f32[1024]{0:T(1024)S(1)}, f32[1024]{0:T(1024)}, u32[]{:S(2)}) copy-start(f32[1024]{0:T(1024)} %copy-done.42) | copy-start | bytes 12292
  671.7 228.8 %reduce-scatter.10.cloned.1.call-start = ((), (), s32[]{:S(2)}) async-start(), calls=%async_computation.15 | async-start | bytes 2949120 | tf_op jit(solution)/shard_map/reduce_scatter | solution.py:294
  671.8 26.1 %copy-start.5 = (bf16[1024,768]{0,1:T(8,128)(2,1)S(1)}, bf16[1024,768]{0,1:T(8,128)(2,1)}, u32[]{:S(2)}) copy-start(bf16[1024,768]{0,1:T(8,128)(2,1)} %copy-done.4) | copy-start | bytes 4718596
  756.0 144.6 %reduce-scatter.12.cloned.1.call-start = ((), (), s32[]{:S(2)}) async-start(), calls=%async_computation.16 | async-start | bytes 2949120 | tf_op jit(solution)/shard_map/reduce_scatter | solution.py:295
  781.7 199.9 %all-gather.18.cloned.1.call-start = ((), (), s32[]{:S(2)}) async-start(), calls=%async_computation.22 | async-start | bytes 10616832 | tf_op jit(solution)/shard_map/all_gather | solution.py:322
  782.3 199.3 %all-gather.16.cloned.1.call-start = ((), (), s32[]{:S(2)}) async-start(), calls=%async_computation.20 | async-start | bytes 10616832 | tf_op jit(solution)/shard_map/all_gather | solution.py:321
  783.0 258.6 %all-reduce.11.cloned.1.call-start = ((), (), s32[]{:S(2)}) async-start(), calls=%async_computation.24 | async-start | bytes 4718592 | tf_op jit(solution)/shard_map/psum | solution.py:303
  816.4 31.0 %copy-start.17 = (bf16[1024,768]{0,1:T(8,128)(2,1)S(1)}, bf16[1024,768]{0,1:T(8,128)(2,1)}, u32[]{:S(2)}) copy-start(bf16[1024,768]{0,1:T(8,128)(2,1)} %get-tuple-element.80) | copy-start | bytes 4718596
  902.0 39.7 %copy-start.47 = (f32[768]{0:T(1024)S(1)}, f32[768]{0:T(1024)}, u32[]{:S(2)}) copy-start(f32[768]{0:T(1024)} %get-tuple-element.60) | copy-start | bytes 9220
  1047.4 10.0 slice-start
  1048.2 9.2 slice-start.1
  1048.2 9.2 slice-start.2
  (34 other events, 90.4 us)
Sparse Core Ops, SparseCore 0:
  9.6 33.3 all-gather.9
  44.5 29.5 all-gather.11
  75.7 29.5 all-gather.7
  106.7 29.5 all-gather.13
  468.2 75.7 reduce-scatter.19
  547.9 76.4 reduce-scatter.17
  627.3 20.5 reduce-scatter.21
  650.3 46.2 reduce-scatter.15
  699.1 47.5 reduce-scatter.13
  756.1 47.1 reduce-scatter.9
  805.7 47.5 reduce-scatter.11
  855.2 58.3 all-gather.17
  915.6 58.7 all-gather.15
  978.2 63.3 all-reduce.10
where the time goes:
time: 1080 us; the launch traced here: 1070 us
  matrix products  387 us (36%)
  local copies, waits for them, and re-layouts  227 us (21%)
  blocking collectives  203 us (19%)
  other arithmetic  121 us (11%)
  waiting for transfers between devices  104 us (10%)
  between operations  17.2 us (2%)
    dot_general x2, matrix products, on_device(): jnp.einsum('vsi,dsi->dv', grad_scores, matches.astype(jnp.float32), preci...  77.7 us
    unnamed x159, local copies, waits for them, and re-layouts  73 us
    mul x2, local copies, waits for them, and re-layouts, on_device(): grad_scores = chances * (grad_chances - inner_sum)  62 us
    dot_general x2, local copies, waits for them, and re-layouts, block_scores(): jnp.einsum('rni,rf->fni', slot_indicators, relative_bias_table, preferred...  60.5 us
    psum x1, waiting for transfers between devices, on_device(): lax.psum((owned_grads[0], owned_grads[1], owned_grads[2], owned_grads[3],...  60 us
    mul x2, other arithmetic, on_device(): grad_scores = chances * (grad_chances - inner_sum)  52 us
    all_gather x1, blocking collectives, on_device(): lax.all_gather(w_router, 'shard', axis=0, tiled=True)  48.8 us
    all_to_all x1, blocking collectives, on_device(): lax.all_to_all(outgoing, 'shard', split_axis=0, concat_axis=1, tiled=True)  44.4 us
  transfers between devices with their start and end apart: 16, of which 2 were waited for; matrix products, arithmetic and copies ran while one was open for 58% of the time, Pallas kernels for 0%

commit v1 on v0

--- a/solution.py
+++ b/solution.py
@@ -167,7 +167,13 @@
     outgoing = jnp.einsum(
         "ect,td->ecd", places, normed_two, preferred_element_type=jnp.float32
     ).astype(jnp.bfloat16)
-    arrived = lax.all_to_all(outgoing, "shard", split_axis=0, concat_axis=1, tiled=True)
+    recover_array_by_axis = lambda local_x, which_dim, join_dim: jnp.concatenate(
+        lax.all_to_all(
+            jnp.stack(jnp.split(local_x, lax.axis_size("shard"), axis=which_dim)), "shard", 0, 0
+        ),
+        axis=join_dim,
+    )
+    arrived = recover_array_by_axis(outgoing, 0, 1)
     before_activation, hidden, result = expert_forward(
         arrived, expert_input_weight, expert_output_weight
     )

time: 1080 us -> 1090 us (level)
  no operation moved by 1% of the time
where the time goes in v1:
time: 1090 us; the launch traced here: 1080 us
  matrix products  386 us (35%)
  local copies, waits for them, and re-layouts  228 us (21%)
  blocking collectives  203 us (19%)
  other arithmetic  131 us (12%)
  waiting for transfers between devices  103 us (9%)
  between operations  17.2 us (2%)
    dot_general x2, matrix products, on_device(): jnp.einsum('vsi,dsi->dv', grad_scores, matches.astype(jnp.float32), preci...  77.7 us
    unnamed x159, local copies, waits for them, and re-layouts  73.2 us
    mul x2, local copies, waits for them, and re-layouts, on_device(): grad_scores = chances * (grad_chances - inner_sum)  62.1 us
    dot_general x2, local copies, waits for them, and re-layouts, block_scores(): jnp.einsum('rni,rf->fni', slot_indicators, relative_bias_table, preferred...  60.8 us
    psum x1, waiting for transfers between devices, on_device(): lax.psum((owned_grads[0], owned_grads[1], owned_grads[2], owned_grads[3],...  59.8 us
    mul x2, other arithmetic, on_device(): grad_scores = chances * (grad_chances - inner_sum)  52 us
    all_gather x1, blocking collectives, on_device(): lax.all_gather(w_router, 'shard', axis=0, tiled=True)  48.8 us
    all_to_all x1, blocking collectives, on_device(): lax.all_to_all(jnp.stack(jnp.split(local_x, lax.axis_size('shard'), axis=...  44.5 us
  transfers between devices with their start and end apart: 16, of which 2 were waited for; matrix products, arithmetic and copies ran while one was open for 58% of the time, Pallas kernels for 0%

profile of v1, /device:TPU:0, one launch (start us, length us, event | category | flops | bytes accessed | tf_op | source)
XLA Modules:
  0.0 1078.1 jit_solution(16910146176125769221)
XLA Ops:
  13.6 13.6 %all-reduce.8 = (bf16[768]{0:T(1024)(128)(2,1)S(1)}, bf16[768]{0:T(1024)(128)(2,1)S(1)}) all-reduce(bf16[768]{0:T(1024)(128)(2,1)S(1)} %dynamic-update-slice, bf16[768]{0:T(1024)(128)(2,1)S(1)} %dynamic-update-slice.1), channel_id=1, replica_groups=mesh['replica'=8,'shard'=4] {'shard'}, use_global_device_ids=true, to_apply=%add | all-reduce | flops 1536 | bytes 6144
  29.9 12.1 %all_gather.42 = bf16[32,12]{1,0:T(8,128)(2,1)S(1)} all-gather(bf16[8,12]{1,0:T(8,128)(2,1)} %param.25), channel_id=1, replica_groups=mesh['replica'=8,'shard'=4] {'shard'}, dimensions={0}, use_global_device_ids=true | all-gather | bytes 960 | tf_op jit(solution)/shard_map/all_gather | solution.py:88
  54.6 16.3 %fusion.1 = f32[512,1024,12]{0,2,1:T(8,128)} fusion(s32[512,1024]{0,1:T(8,128)S(1)} %fusion.85, bf16[32,12]{1,0:T(8,128)(2,1)S(1)} %all_gather.42), kind=kOutput, calls=%fused_computation.2 | convolution fusion | flops 419430400 | bytes 27263744 | tf_op jit(solution)/shard_map/rni,rf->fni/dot_general | solution.py:31
  70.9 30.2 %copy.81 = f32[512,1024,12]{1,0,2:T(8,128)} copy(f32[512,1024,12]{0,2,1:T(8,128)} %fusion.1) | data formatting | bytes 50331648 | tf_op jit(solution)/shard_map/rni,rf->fni/dot_general | solution.py:31
  101.1 16.6 %fusion.3 = f32[512,1024,12]{0,2,1:T(8,128)} fusion(s32[512,1024]{0,1:T(8,128)S(1)} %fusion.84, bf16[32,12]{1,0:T(8,128)(2,1)S(1)} %all_gather.42), kind=kOutput, calls=%fused_computation.5 | convolution fusion | flops 419430400 | bytes 27263744 | tf_op jit(solution)/shard_map/rni,rf->fni/dot_general | solution.py:31
  117.7 30.6 %copy.80 = f32[512,1024,12]{1,0,2:T(8,128)} copy(f32[512,1024,12]{0,2,1:T(8,128)} %fusion.3) | data formatting | bytes 50331648 | tf_op jit(solution)/shard_map/rni,rf->fni/dot_general | solution.py:31
  156.6 16.6 %fusion.161 = (f32[12,512]{1,0:T(8,128)S(1)}, f32[12,512,1024]{2,1,0:T(8,128)}) fusion(f32[512,1024,12]{1,0,2:T(8,128)} %copy.81, bf16[1024,12,64]{0,2,1:T(8,128)(2,1)S(1)} %bitcast.178, bf16[1,1024,12,64]{1,3,2,0:T(8,128)(2,1)} %bitcast.198, pred[512,1024]{1,0:T(8,128)(4,1)} %get-tuple-element.86), kind=kOutput, calls=%fused_computation.204 | convolution fusion | flops 824174592 | bytes 53239808 | tf_op jit(solution)/shard_map/qhe,khe->hqk/dot_general | solution.py:30
  173.2 20.4 %fusion.11 = f32[12,512]{1,0:T(8,128)S(1)} fusion(f32[12,512,1024]{2,1,0:T(8,128)} %get-tuple-element.92, f32[12,512]{1,0:T(8,128)S(1)} %get-tuple-element.91), kind=kLoop, calls=%fused_computation.27 | loop fusion | flops 12576768 | bytes 25214976 | tf_op jit(solution)/shard_map/reduce_sum | solution.py:141
  196.5 11.9 %fusion.133 = bf16[512,12,64]{0,2,1:T(8,128)(2,1)} fusion(bf16[1024,12,64]{0,2,1:T(8,128)(2,1)S(1)} %bitcast.188, f32[12,512,1024]{2,1,0:T(8,128)} %get-tuple-element.92, f32[12,512]{1,0:T(8,128)S(1)} %fusion.11, f32[12,512]{1,0:T(8,128)S(1)} %get-tuple-element.91), kind=kOutput, calls=%fused_computation.152 | convolution fusion | flops 824573952 | bytes 27574272 | tf_op jit(solution)/shard_map/hqk,khe->qhe/dot_general | solution.py:145
  208.5 15.7 %fusion.162 = (f32[12,512]{1,0:T(8,128)S(1)}, f32[12,512,1024]{2,1,0:T(8,128)}) fusion(f32[512,1024,12]{1,0,2:T(8,128)} %copy.80, bf16[1024,12,64]{0,2,1:T(8,128)(2,1)S(1)} %bitcast.179, bf16[1,1024,12,64]{1,3,2,0:T(8,128)(2,1)S(1)} %bitcast.199, pred[512,1024]{1,0:T(8,128)(4,1)} %get-tuple-element.85), kind=kOutput, calls=%fused_computation.205 | convolution fusion | flops 824174592 | bytes 53239808 | tf_op jit(solution)/shard_map/qhe,khe->hqk/dot_general | solution.py:30
  224.2 11.0 %fusion.10 = f32[12,512]{1,0:T(8,128)S(1)} fusion(f32[12,512,1024]{2,1,0:T(8,128)} %get-tuple-element.94, f32[12,512]{1,0:T(8,128)S(1)} %get-tuple-element.93), kind=kLoop, calls=%fused_computation.26 | loop fusion | flops 12576768 | bytes 25214976 | tf_op jit(solution)/shard_map/reduce_sum | solution.py:141
  235.2 10.5 fusion.132
  254.8 44.5 %all_to_all.38 = bf16[4,1,320,768]{3,2,1,0:T(8,128)(2,1)S(1)} all-to-all(bf16[4,1,320,768]{3,2,1,0:T(8,128)(2,1)S(1)} %pad_maximum_fusion), channel_id=1, replica_groups=mesh['replica'=8,'shard'=4] {'shard'}, dimensions={0} | all-to-all | bytes 3932160 | tf_op jit(solution)/shard_map/all_to_all | solution.py:171
  300.6 6.4 fusion.51
  307.1 9.6 fusion.70
  316.8 15.1 %copy.116 = bf16[1,1280,768]{2,0,1:T(2,128)(2,1)} copy(bf16[1,1280,768]{2,1,0:T(8,128)(2,1)S(1)} %fusion.70) | data formatting | bytes 3932160 | tf_op jit(solution)/shard_map/convert_element_type | solution.py:45
  332.3 13.7 %reduce.2 = bf16[1280,768]{1,0:T(8,128)(2,1)} reduce(bf16[1280,1,768]{2,1,0:T(2,128)(2,1)} %bitcast.182, bf16[]{:T(256)} %broadcast.378), dimensions={1}, to_apply=%bitcast.176.reduce_sub_computation | reduce | bytes 3932162
  350.0 4.5 all-to-all-start.1
  354.5 48.8 %all-gather = bf16[4,192,4]{1,2,0:T(4,128)(2,1)S(1)} all-gather(bf16[1,192,4]{1,2,0:T(4,128)(2,1)S(1)} %bitcast.224), channel_id=1, replica_groups=mesh['replica'=8,'shard'=4] {'shard'}, dimensions={0}, use_global_device_ids=true | all-gather | bytes 7680 | tf_op jit(solution)/shard_map/all_gather | solution.py:87
  408.1 4.8 reshape.407
  422.3 44.4 %all_to_all.39 = bf16[4,320,768]{2,1,0:T(8,128)(2,1)S(1)} all-to-all(bf16[4,320,768]{2,1,0:T(8,128)(2,1)S(1)} %fusion.107), channel_id=1, replica_groups=mesh['replica'=8,'shard'=4] {'shard'}, dimensions={0} | all-to-all | bytes 3932160 | tf_op jit(solution)/shard_map/all_to_all | solution.py:212
  468.0 10.0 convolution_bitcast_fusion
  478.1 18.7 %fusion.20 = bf16[1280,3072]{1,0:T(8,128)(2,1)S(1)} fusion(f32[1280,3072]{1,0:T(8,128)} %copy-done.54, bf16[1280,768]{1,0:T(8,128)(2,1)} %bitcast.205, bf16[1,3072,768]{2,1,0:T(8,128)(2,1)} %param.27), kind=kOutput, calls=%fused_computation.36 | convolution fusion | flops 6118440960 | bytes 30277632 | tf_op jit(solution)/shard_map/ecd,efd->ecf/dot_general | solution.py:50
  500.0 8.8 convolution_bitcast_fusion.1
  508.8 10.4 fusion.73
  519.2 15.3 %copy.115 = bf16[1,1280,768]{2,0,1:T(2,128)(2,1)} copy(bf16[1,1280,768]{2,1,0:T(8,128)(2,1)S(1)} %fusion.73) | data formatting | bytes 3932160 | tf_op jit(solution)/shard_map/convert_element_type | solution.py:60
  534.5 13.8 %reduce.3 = bf16[1280,768]{1,0:T(8,128)(2,1)} reduce(bf16[1280,1,768]{2,1,0:T(2,128)(2,1)} %bitcast.183, bf16[]{:T(256)} %broadcast.378), dimensions={1}, to_apply=%bitcast.175.reduce_sub_computation | reduce | bytes 3932162
  552.2 4.4 all-to-all-start.3
  560.4 39.6 %all-to-all-done.3 = bf16[4,2,122880]{2,1,0:T(2,128)(2,1)} async-done(((bf16[4,2,122880]{2,1,0:T(2,128)(2,1)}), bf16[4,2,122880]{2,1,0:T(2,128)(2,1)}, u32[]{:S(2)}, u32[]{:S(2)}) %all-to-all-start.3) | async-done | bytes 1966112 | tf_op jit(solution)/shard_map/all_to_all | solution.py:216
  600.0 5.2 reshape.409
  623.3 11.1 %fusion.21 = f32[12,64,1024]{2,1,0:T(8,128)S(1)} fusion(f32[12,512,1024]{2,1,0:T(8,128)} %get-tuple-element.92, f32[12,512]{1,0:T(8,128)S(1)} %log_add_fusion, bf16[1,1024,12,64]{1,3,2,0:T(8,128)(2,1)S(1)} %bitcast.194), kind=kOutput, calls=%fused_computation.38 | convolution fusion | flops 817889280 | bytes 29130752 | tf_op jit(solution)/shard_map/hqk,qhe->khe/dot_general | solution.py:251
  634.5 10.7 add_convert_fusion
  649.2 16.2 %multiply_reduce_fusion = (f32[12,512]{1,0:T(8,128)S(1)}, f32[12,512,1024]{2,1,0:T(8,128)}) fusion(f32[12,512,1024]{2,1,0:T(8,128)} %get-tuple-element.92, f32[12,512]{1,0:T(8,128)S(1)} %log_add_fusion, bf16[1024,12,64]{0,2,1:T(8,128)(2,1)S(1)} %bitcast.190, bf16[1,1024,12,64]{1,3,2,0:T(8,128)(2,1)} %bitcast.196), kind=kOutput, calls=%fused_computation.15 | convolution fusion | flops 824174592 | bytes 52740096 | tf_op jit(solution)/shard_map/qhe,khe->hqk/dot_general | solution.py:257
  665.4 16.0 %multiply_reduce_fusion.1 = (f32[12,512]{1,0:T(8,128)S(1)}, f32[12,512,1024]{2,1,0:T(8,128)}) fusion(f32[12,512,1024]{2,1,0:T(8,128)} %get-tuple-element.94, f32[12,512]{1,0:T(8,128)S(1)} %log_add_fusion.1, bf16[1024,12,64]{0,2,1:T(8,128)(2,1)S(1)} %bitcast.191, bf16[1,1024,12,64]{1,3,2,0:T(8,128)(2,1)} %bitcast.197), kind=kOutput, calls=%fused_computation.18 | convolution fusion | flops 824174592 | bytes 52740096 | tf_op jit(solution)/shard_map/qhe,khe->hqk/dot_general | solution.py:257
  681.5 26.0 %subtract_multiply_fusion = f32[12,512,1024]{2,1,0:T(8,128)} fusion(f32[12,512,1024]{2,1,0:T(8,128)} %get-tuple-element.103, f32[12,512,1024]{2,1,0:T(8,128)} %get-tuple-element.92, f32[12,512]{1,0:T(8,128)S(1)} %get-tuple-element.102, f32[12,512]{1,0:T(8,128)S(1)} %log_add_fusion), kind=kLoop, calls=%fused_computation.14 | loop fusion | flops 18874368 | bytes 75546624 | tf_op jit(solution)/shard_map/mul | solution.py:261
  707.5 13.4 %fusion.126 = bf16[512,12,64]{0,2,1:T(8,128)(2,1)} fusion(bf16[1024,12,64]{0,2,1:T(8,128)(2,1)S(1)} %bitcast.180, f32[12,512,1024]{2,1,0:T(8,128)} %subtract_multiply_fusion), kind=kOutput, calls=%fused_computation.149 | convolution fusion | flops 811991040 | bytes 27525120 | tf_op jit(solution)/shard_map/hqk,khe->qhe/dot_general | solution.py:271
  720.9 26.0 %subtract_multiply_fusion.1 = f32[12,512,1024]{2,1,0:T(8,128)} fusion(f32[12,512,1024]{2,1,0:T(8,128)} %get-tuple-element.105, f32[12,512,1024]{2,1,0:T(8,128)} %get-tuple-element.94, f32[12,512]{1,0:T(8,128)S(1)} %get-tuple-element.104, f32[12,512]{1,0:T(8,128)S(1)} %log_add_fusion.1), kind=kLoop, calls=%fused_computation.17 | loop fusion | flops 18874368 | bytes 75546624 | tf_op jit(solution)/shard_map/mul | solution.py:261
  746.9 13.1 %fusion.129 = bf16[512,12,64]{0,2,1:T(8,128)(2,1)} fusion(bf16[1024,12,64]{0,2,1:T(8,128)(2,1)S(1)} %bitcast.181, f32[12,512,1024]{2,1,0:T(8,128)} %subtract_multiply_fusion.1), kind=kOutput, calls=%fused_computation.150 | convolution fusion | flops 811991040 | bytes 27525120 | tf_op jit(solution)/shard_map/hqk,khe->qhe/dot_general | solution.py:271
  765.7 10.9 %fusion.29 = f32[12,64,1024]{2,1,0:T(8,128)S(1)} fusion(f32[12,512,1024]{2,1,0:T(8,128)} %subtract_multiply_fusion, bf16[1,1024,12,64]{1,3,2,0:T(8,128)(2,1)S(1)} %bitcast.200), kind=kOutput, calls=%fused_computation.44 | convolution fusion | flops 811597824 | bytes 29097984 | tf_op jit(solution)/shard_map/hqk,qhe->khe/dot_general | solution.py:275
  776.6 10.7 add_convert_fusion.1
  795.0 31.1 %copy.94 = f32[12,512,1024]{1,0,2:T(8,128)} copy(f32[12,512,1024]{2,1,0:T(8,128)} %subtract_multiply_fusion) | data formatting | bytes 50331648 | tf_op jit(solution)/shard_map/mul | solution.py:261
  826.1 31.0 %copy.93 = f32[12,512,1024]{1,0,2:T(8,128)} copy(f32[12,512,1024]{2,1,0:T(8,128)} %subtract_multiply_fusion.1) | data formatting | bytes 50331648 | tf_op jit(solution)/shard_map/mul | solution.py:261
  872.1 38.0 %fusion.134 = f32[32,12]{1,0:T(8,128)S(1)} fusion(f32[12,512,1024]{1,0,2:T(8,128)} %copy.93, s32[512,1024]{0,1:T(8,128)S(1)} %copy-done.3), kind=kOutput, calls=%fused_computation.153 | convolution fusion | flops 2432696320 | bytes 27264512 | tf_op jit(solution)/shard_map/vsi,dsi->dv/dot_general | solution.py:262
  911.7 39.7 %fusion.136 = f32[32,12]{1,0:T(8,128)S(1)} fusion(f32[32,12]{1,0:T(8,128)S(1)} %fusion.134, f32[12,512,1024]{1,0,2:T(8,128)} %copy.94, s32[512,1024]{0,1:T(8,128)S(1)} %copy-done.1), kind=kOutput, calls=%fused_computation.155 | convolution fusion | flops 2432696832 | bytes 27266048 | tf_op jit(solution)/shard_map/vsi,dsi->dv/dot_general | solution.py:262
  951.5 17.3 %all-reduce.7 = (f32[768]{0:T(1024)S(1)}, f32[768]{0:T(1024)S(1)}, f32[32,12]{1,0:T(8,128)S(1)}) all-reduce(f32[768]{0:T(1024)S(1)} %get-tuple-element.62, f32[768]{0:T(1024)S(1)} %copy-done.47, f32[32,12]{1,0:T(8,128)S(1)} %fusion.136), channel_id=6, replica_groups=mesh['replica'=8,'shard'=4] {'shard'}, use_global_device_ids=true, to_apply=%region_26.27.clone | all-reduce | flops 1920 | bytes 15360
  968.9 22.7 %all-reduce.5 = (f32[192]{0:T(256)}, f32[192]{0:T(256)}, f32[192,4]{0,1:T(4,128)}, f32[8,12]{1,0:T(8,128)}) all-reduce(f32[192]{0:T(256)S(1)} %dynamic-slice.3, f32[192]{0:T(256)S(1)} %dynamic-slice.5, f32[192,4]{0,1:T(4,128)S(1)} %copy.108, ...), channel_id=1, replica_groups=mesh['replica'=8,'shard'=4] {'replica'}, use_global_device_ids=true, to_apply=%region_27.28 | all-reduce | flops 1248 | bytes 9984 | tf_op jit(solution)/shard_map/psum | solution.py:309
  991.7 59.8 %all-reduce.11.cloned.1.call-done = (f32[192,768]{1,0:T(8,128)}, f32[192,768]{1,0:T(8,128)}, f32[192,768]{1,0:T(8,128)}, f32[192,768]{1,0:T(8,128)}) async-done(((f32[192,768]{1,0:T(8,128)}, f32[192,768]{1,0:T(8,128)}, f32[192,768]{1,0:T(8,128)}, f32[192,768]{1,0:T(8,128)}), (f32[192,768]{1,0:T(8,128)}, f32[192,768]{1,0:T(8,128)}, f32[192,768]{1,0:T(8,128)}, ...) | async-done | bytes 2359312 | tf_op jit(solution)/shard_map/psum | solution.py:309
  1058.1 9.2 copy.129
  (257 shorter events, 134.4 us)
Async XLA Ops:
  7.2 142.7 %all-gather.10.cloned.1.call-start = ((), (), s32[]{:S(2)}) async-start(), calls=%async_computation.12 | async-start | bytes 1474560 | tf_op jit(solution)/shard_map/all_gather | solution.py:81
  7.9 145.9 %all-gather.12.cloned.1.call-start = ((), (), s32[]{:S(2)}) async-start(), calls=%async_computation.13 | async-start | bytes 1474560 | tf_op jit(solution)/shard_map/all_gather | solution.py:82
  8.7 185.0 %all-gather.8.cloned.1.call-start = ((), (), s32[]{:S(2)}) async-start(), calls=%async_computation.11 | async-start | bytes 1474560 | tf_op jit(solution)/shard_map/all_gather | solution.py:83
  9.4 237.7 %all-gather.14.cloned.1.call-start = ((), (), s32[]{:S(2)}) async-start(), calls=%async_computation.14 | async-start | bytes 1474560 | tf_op jit(solution)/shard_map/all_gather | solution.py:84
  27.3 166.4 %copy-start.40 = (f32[768]{0:T(1024)}, f32[768]{0:T(1024)S(1)}, u32[]{:S(2)}) copy-start(f32[768]{0:T(1024)S(1)} %convert_element_type.284) | copy-start | bytes 9220
  49.1 144.6 %copy-start.42 = (f32[1024]{0:T(1024)}, f32[1024]{0:T(1024)S(1)}, u32[]{:S(2)}) copy-start(f32[1024]{0:T(1024)S(1)} %fusion.146) | copy-start | bytes 12292
  51.2 49.9 %copy-start.2 = (s32[512,1024]{0,1:T(8,128)}, s32[512,1024]{0,1:T(8,128)S(1)}, u32[]{:S(2)}) copy-start(s32[512,1024]{0,1:T(8,128)S(1)} %fusion.84) | copy-start | bytes 6291460
  117.7 30.6 %copy-start.46 = (s32[1,1024]{1,0:T(1,128)S(1)}, s32[1,1024]{1,0:T(1,128)}, u32[]{:S(2)}) copy-start(s32[1,1024]{1,0:T(1,128)} %param.16) | copy-start | bytes 12292
  117.7 32.3 %copy-start.7 = (bf16[1024,768]{0,1:T(8,128)(2,1)S(1)}, bf16[1024,768]{0,1:T(8,128)(2,1)}, u32[]{:S(2)}) copy-start(bf16[1024,768]{0,1:T(8,128)(2,1)} %copy-done.6) | copy-start | bytes 4718596
  156.6 51.8 %copy-start.4 = (bf16[1024,768]{0,1:T(8,128)(2,1)}, bf16[1024,768]{0,1:T(8,128)(2,1)S(1)}, u32[]{:S(2)}) copy-start(bf16[1024,768]{0,1:T(8,128)(2,1)S(1)} %convolution_convert_fusion.1) | copy-start | bytes 4718596
  173.2 23.3 %copy-start.34 = (f32[12,512]{1,0:T(8,128)}, f32[12,512]{1,0:T(8,128)S(1)}, u32[]{:S(2)}) copy-start(f32[12,512]{1,0:T(8,128)S(1)} %get-tuple-element.91) | copy-start | bytes 73732
  196.5 12.0 %copy-start.12 = (bf16[1024,768]{0,1:T(8,128)(2,1)}, bf16[1024,768]{0,1:T(8,128)(2,1)S(1)}, u32[]{:S(2)}) copy-start(bf16[1024,768]{0,1:T(8,128)(2,1)S(1)} %convolution_convert_fusion.3) | copy-start | bytes 4718596
  196.5 12.0 %copy-start.21 = (bf16[1024,768]{0,1:T(8,128)(2,1)S(1)}, bf16[1024,768]{0,1:T(8,128)(2,1)}, u32[]{:S(2)}) copy-start(bf16[1024,768]{0,1:T(8,128)(2,1)} %convolution_convert_fusion.2) | copy-start | bytes 4718596
  224.2 11.0 %copy-start.13 = (bf16[1024,768]{0,1:T(8,128)(2,1)S(1)}, bf16[1024,768]{0,1:T(8,128)(2,1)}, u32[]{:S(2)}) copy-start(bf16[1024,768]{0,1:T(8,128)(2,1)} %copy-done.12) | copy-start | bytes 4718596
  235.2 10.5 copy-start.32
  247.1 53.5 %slice-start.5 = ((s8[4718592]{0:T(1024)(128)(4,1)}), s8[4194304]{0:T(1024)(128)(4,1)S(1)}, s32[]{:S(2)}) async-start(s8[4718592]{0:T(1024)(128)(4,1)} %bitcast.227), calls=%async_computation.30 | async-start | bytes 8388608
  251.7 48.9 %slice-start.6 = ((s8[4718592]{0:T(1024)(128)(4,1)}), s8[524288]{0:T(1024)(128)(4,1)S(1)}, s32[]{:S(2)}) async-start(s8[4718592]{0:T(1024)(128)(4,1)} %bitcast.227), calls=%async_computation.31 | async-start | bytes 1048576
  254.5 52.5 %slice-start.3 = ((s8[4718592]{0:T(1024)(128)(4,1)}), s8[4194304]{0:T(1024)(128)(4,1)S(1)}, s32[]{:S(2)}) async-start(s8[4718592]{0:T(1024)(128)(4,1)} %bitcast.225), calls=%async_computation.28 | async-start | bytes 8388608
  307.1 9.6 copy-start.54
  346.1 8.4 copy-start.50
  350.0 58.1 %all-to-all-start.1 = ((bf16[4,2,122880]{2,1,0:T(2,128)(2,1)}), bf16[4,2,122880]{2,1,0:T(2,128)(2,1)}, u32[]{:S(2)}, u32[]{:S(2)}) async-start(bf16[4,2,122880]{2,1,0:T(2,128)(2,1)} %reshape.406), calls=%async_computation.1 | async-start | bytes 3932160 | tf_op jit(solution)/shard_map/all_to_all | solution.py:180
  354.4 437.0 %reduce-scatter.20.cloned.1.call-start = ((), (), s32[]{:S(2)}) async-start(), calls=%async_computation.21 | async-start | bytes 10616832 | tf_op jit(solution)/shard_map/reduce_scatter | solution.py:324
  415.5 52.5 %slice-start.7 = ((s8[15728640]{0:T(1024)(128)(4,1)}), s8[4194304]{0:T(1024)(128)(4,1)S(1)}, s32[]{:S(2)}) async-start(s8[15728640]{0:T(1024)(128)(4,1)} %bitcast.229), calls=%async_computation.32 | async-start | bytes 8388608
  415.5 52.5 %slice-start.8 = ((s8[15728640]{0:T(1024)(128)(4,1)}), s8[4194304]{0:T(1024)(128)(4,1)S(1)}, s32[]{:S(2)}) async-start(s8[15728640]{0:T(1024)(128)(4,1)} %bitcast.229), calls=%async_computation.33 | async-start | bytes 8388608
  419.6 48.4 %slice-start.9 = ((s8[15728640]{0:T(1024)(128)(4,1)}), s8[4194304]{0:T(1024)(128)(4,1)S(1)}, s32[]{:S(2)}) async-start(s8[15728640]{0:T(1024)(128)(4,1)} %bitcast.229), calls=%async_computation.34 | async-start | bytes 8388608
  419.6 48.4 %slice-start.10 = ((s8[15728640]{0:T(1024)(128)(4,1)}), s8[3145728]{0:T(1024)(128)(4,1)S(1)}, s32[]{:S(2)}) async-start(s8[15728640]{0:T(1024)(128)(4,1)} %bitcast.229), calls=%async_computation.35 | async-start | bytes 6291456
  478.0 313.9 %reduce-scatter.18.cloned.1.call-start = ((), (), s32[]{:S(2)}) async-start(), calls=%async_computation.19 | async-start | bytes 10616832 | tf_op jit(solution)/shard_map/reduce_scatter | solution.py:323
  478.1 21.9 %copy-start.25 = (bf16[4,1,320,768]{3,2,1,0:T(8,128)(2,1)S(1)}, bf16[4,1,320,768]{3,2,1,0:T(8,128)(2,1)}, u32[]{:S(2)}) copy-start(bf16[4,1,320,768]{3,2,1,0:T(8,128)(2,1)} %copy-done.24) | copy-start | bytes 5898244
  548.3 8.4 copy-start.38
  552.2 47.7 %all-to-all-start.3 = ((bf16[4,2,122880]{2,1,0:T(2,128)(2,1)}), bf16[4,2,122880]{2,1,0:T(2,128)(2,1)}, u32[]{:S(2)}, u32[]{:S(2)}) async-start(bf16[4,2,122880]{2,1,0:T(2,128)(2,1)} %reshape.408), calls=%async_computation.3 | async-start | bytes 3932160 | tf_op jit(solution)/shard_map/all_to_all | solution.py:216
  556.6 237.4 %reduce-scatter.22.cloned.1.call-start = ((), (), s32[]{:S(2)}) async-start(), calls=%async_computation.23 | async-start | bytes 491520
  560.3 349.8 %reduce-scatter.16.cloned.1.call-start = ((), (), s32[]{:S(2)}) async-start(), calls=%async_computation.18 | async-start | bytes 2949120 | tf_op jit(solution)/shard_map/reduce_scatter | solution.py:303
  619.9 290.3 %reduce-scatter.14.cloned.1.call-start = ((), (), s32[]{:S(2)}) async-start(), calls=%async_computation.17 | async-start | bytes 2949120 | tf_op jit(solution)/shard_map/reduce_scatter | solution.py:302
  623.3 11.2 %copy-start.20 = (bf16[1024,768]{0,1:T(8,128)(2,1)}, bf16[1024,768]{0,1:T(8,128)(2,1)S(1)}, u32[]{:S(2)}) copy-start(bf16[1024,768]{0,1:T(8,128)(2,1)S(1)} %convolution_convert_fusion) | copy-start | bytes 4718596
  634.4 11.9 %copy-start.8 = (bf16[1024,768]{0,1:T(8,128)(2,1)S(1)}, bf16[1024,768]{0,1:T(8,128)(2,1)}, u32[]{:S(2)}) copy-start(bf16[1024,768]{0,1:T(8,128)(2,1)} %copy-done.6) | copy-start | bytes 4718596
  634.4 11.9 %copy-start.41 = (f32[768]{0:T(1024)S(1)}, f32[768]{0:T(1024)}, u32[]{:S(2)}) copy-start(f32[768]{0:T(1024)} %copy-done.40) | copy-start | bytes 9220
  634.4 11.9 %copy-start.43 = (f32[1024]{0:T(1024)S(1)}, f32[1024]{0:T(1024)}, u32[]{:S(2)}) copy-start(f32[1024]{0:T(1024)} %copy-done.42) | copy-start | bytes 12292
  681.4 228.8 %reduce-scatter.10.cloned.1.call-start = ((), (), s32[]{:S(2)}) async-start(), calls=%async_computation.15 | async-start | bytes 2949120 | tf_op jit(solution)/shard_map/reduce_scatter | solution.py:300
  681.5 26.0 %copy-start.5 = (bf16[1024,768]{0,1:T(8,128)(2,1)S(1)}, bf16[1024,768]{0,1:T(8,128)(2,1)}, u32[]{:S(2)}) copy-start(bf16[1024,768]{0,1:T(8,128)(2,1)} %copy-done.4) | copy-start | bytes 4718596
  765.6 144.7 %reduce-scatter.12.cloned.1.call-start = ((), (), s32[]{:S(2)}) async-start(), calls=%async_computation.16 | async-start | bytes 2949120 | tf_op jit(solution)/shard_map/reduce_scatter | solution.py:301
  791.3 200.3 %all-gather.18.cloned.1.call-start = ((), (), s32[]{:S(2)}) async-start(), calls=%async_computation.22 | async-start | bytes 10616832 | tf_op jit(solution)/shard_map/all_gather | solution.py:328
  791.9 199.8 %all-gather.16.cloned.1.call-start = ((), (), s32[]{:S(2)}) async-start(), calls=%async_computation.20 | async-start | bytes 10616832 | tf_op jit(solution)/shard_map/all_gather | solution.py:327
  792.6 258.8 %all-reduce.11.cloned.1.call-start = ((), (), s32[]{:S(2)}) async-start(), calls=%async_computation.24 | async-start | bytes 4718592 | tf_op jit(solution)/shard_map/psum | solution.py:309
  826.1 31.0 %copy-start.17 = (bf16[1024,768]{0,1:T(8,128)(2,1)S(1)}, bf16[1024,768]{0,1:T(8,128)(2,1)}, u32[]{:S(2)}) copy-start(bf16[1024,768]{0,1:T(8,128)(2,1)} %get-tuple-element.80) | copy-start | bytes 4718596
  911.7 39.7 %copy-start.47 = (f32[768]{0:T(1024)S(1)}, f32[768]{0:T(1024)}, u32[]{:S(2)}) copy-start(f32[768]{0:T(1024)} %get-tuple-element.60) | copy-start | bytes 9220
  1057.3 10.0 slice-start
  1058.1 9.2 slice-start.1
  1058.1 9.2 slice-start.2
  (34 other events, 90.4 us)
Sparse Core Ops, SparseCore 0:
  9.6 33.3 all-gather.9
  44.5 29.5 all-gather.11
  75.7 29.5 all-gather.7
  106.7 29.5 all-gather.13
  478.2 75.7 reduce-scatter.19
  557.9 76.4 reduce-scatter.17
  637.2 20.5 reduce-scatter.21
  660.3 46.3 reduce-scatter.15
  709.0 47.5 reduce-scatter.13
  765.7 47.3 reduce-scatter.9
  815.5 47.5 reduce-scatter.11
  865.0 58.3 all-gather.17
  925.4 58.7 all-gather.15
  988.0 63.4 all-reduce.10
